TPU v7x, 32 devices: a whole 2x2x4 slice. The times are simulated.
32 devices in a mesh: dp: 8 (over z, x), tensor: 4 (over y, core).
Axes of the slice: x: 2, y: 2, z: 4, core: 2. Of those that a mesh axis runs over, the one named last changes fastest.
Arguments:
- tokens: bfloat16 [4096, 1024], P(('dp', 'tensor')), may hold values from -6 to 6
- segment_ids: int32 [8, 512], P('dp'), may hold values from 0 to 2, as said below
- positions: int32 [8, 512], P('dp'), may hold values from 0 to 511, as said below
- norm_in_gain: float32 [1024], replicated, may hold values from 0.5 to 1.5
- w_query: bfloat16 [1024, 1024], P('dp', 'tensor'), may hold values from -0.1875 to 0.1875
- w_key: bfloat16 [1024, 512], P('dp', 'tensor'), may hold values from -0.1875 to 0.1875
- w_value: bfloat16 [1024, 512], P('dp', 'tensor'), may hold values from -0.1875 to 0.1875
- query_gain: float32 [64], replicated, may hold values from 0.1 to 1.9
- key_gain: float32 [64], replicated, may hold values from 0.1 to 1.9
- w_output: bfloat16 [1024, 1024], P('tensor', 'dp'), may hold values from -0.75 to 0.75
- norm_mid_gain: float32 [1024], replicated, may hold values from 0.5 to 1.5
- w_gate: bfloat16 [1024, 4608], P('dp', 'tensor'), may hold values from -0.1875 to 0.1875
- w_up: bfloat16 [1024, 4608], P('dp', 'tensor'), may hold values from -0.1875 to 0.1875
- w_down: bfloat16 [4608, 1024], P('tensor', 'dp'), may hold values from -0.125 to 0.125
- grad_out: bfloat16 [4096, 1024], P(('dp', 'tensor')), may hold values from -6 to 6
Outputs:
- block_out: bfloat16 [4096, 1024], P(('dp', 'tensor'))
- grad_tokens: bfloat16 [4096, 1024], P(('dp', 'tensor'))
- grad_norm_in: float32 [1024], replicated
- grad_w_query: float32 [1024, 1024], P('dp', 'tensor')
- grad_w_key: float32 [1024, 512], P('dp', 'tensor')
- grad_w_value: float32 [1024, 512], P('dp', 'tensor')
- grad_query_gain: float32 [64], replicated
- grad_key_gain: float32 [64], replicated
- grad_w_output: float32 [1024, 1024], P('tensor', 'dp')
- grad_norm_mid: float32 [1024], replicated
- grad_w_gate: float32 [1024, 4608], P('dp', 'tensor')
- grad_w_up: float32 [1024, 4608], P('dp', 'tensor')
- grad_w_down: float32 [4608, 1024], P('tensor', 'dp')
Inputs may be any that keep to these rules, and one draw needn't show every extreme that they name: `segment_ids`: within each sequence document numbers start at 0, never fall and rise by one at each new document; each sequence holds one to three documents, and one of them covers more than half of it; some sequence holds three. `positions`: each token's index within its document, counted from 0 at the document's first token; some sequence is a single document.
All inputs are finite; a program needn't handle non-finite values.
Results may differ from a plain program's by a relative error of at most 0.02.
Values may be sent and summed in bfloat16 or wider, within the bound.
No kernel may reach another device: no remote copies, remote signals or barrier semaphores. Data moves between devices by JAX's collectives and lax.ppermute only.
A program may use at most 128 MiB of HBM per device.

v0:
```python
import jax
import jax.numpy as jnp
from jax import lax
from jax.sharding import PartitionSpec as P

EPSILON = 1e-05
AXES = ("dp", "tensor")
LOW = jnp.bfloat16
FULL = jnp.float32
LANES = 128


def matmul(left, right):
    return jnp.dot(left, right, preferred_element_type=FULL)


def matmul_back(left, right):
    return lax.dot_general(left, right, (((1,), (1,)), ((), ())), preferred_element_type=FULL)


def matmul_rows(left, right):
    return lax.dot_general(left, right, (((0,), (0,)), ((), ())), preferred_element_type=FULL)


def scale_of(values):
    return lax.rsqrt(jnp.mean(values * values, axis=-1, keepdims=True) + EPSILON)


def normalize(values, gain):
    return values * scale_of(values) * gain


def normalize_back(values, gain, grad):
    scale = scale_of(values)
    grad = grad * gain
    inner = jnp.mean(grad * values, axis=-1, keepdims=True)
    return scale * grad - values * (scale * scale * scale * inner)


def angles_of(places, width):
    half = width // 2
    steps = jnp.arange(half, dtype=FULL) * (2.0 / width)
    freqs = jnp.power(jnp.float32(1000000.0), -steps)
    angles = places.astype(FULL)[:, None] * freqs[None, :]
    return jnp.cos(angles)[:, None, :], jnp.sin(angles)[:, None, :]


def rotate(values, cosine, sine):
    half = values.shape[-1] // 2
    first = values[..., :half]
    second = values[..., half:]
    return jnp.concatenate(
        [first * cosine - second * sine, second * cosine + first * sine], axis=-1
    )


def pick(array, index, axis):
    return lax.dynamic_index_in_dim(array, index, axis, keepdims=False)


def ordered(mine, other, bit, axis):
    first = bit == 0
    return jnp.stack([jnp.where(first, mine, other), jnp.where(first, other, mine)], axis=axis)


def after(array, *others):
    return lax.optimization_barrier((array,) + others)[0]


class Plan:
    def __init__(self, mesh):
        self.dp = mesh.shape["dp"]
        self.tensor = mesh.shape["tensor"]
        self.devices = self.dp * self.tensor
        self.lines = self.dp // 2
        self.stride = 2 * self.tensor
        self.core_mask = 1
        self.row_mask = self.tensor // 2
        self.pair_mask = self.tensor

    def here(self):
        dp = lax.axis_index("dp")
        tensor = lax.axis_index("tensor")
        self.line = dp // 2
        self.pair = dp % 2
        self.row = tensor // 2
        self.core = tensor % 2

    def swap(self, array, mask):
        return lax.ppermute(array, AXES, [(i, i ^ mask) for i in range(self.devices)])

    def groups(self):
        return [
            [line * 2 + pair for line in range(self.lines)] for pair in range(2)
        ]

    def gather_lines(self, array):
        return lax.all_gather(array, "dp", axis=0, tiled=True, axis_index_groups=self.groups())

    def sum_lines(self, parts):
        return lax.psum_scatter(
            parts, "dp", scatter_dimension=0, tiled=True, axis_index_groups=self.groups()
        )

    def gather_lines_direct(self, array):
        count = self.lines
        if count > 4:
            return lax.all_gather(array, "dp", axis=0, axis_index_groups=self.groups())
        whole = lax.dynamic_update_index_in_dim(
            jnp.zeros((count,) + array.shape, array.dtype), array, self.line, 0
        )
        others = [self.swap(array, away * self.stride) for away in range(1, count)]
        for away, other in enumerate(others, 1):
            whole = lax.dynamic_update_index_in_dim(whole, other, self.line ^ away, 0)
        return whole

    def sum_lines_direct(self, parts):
        count = self.lines
        if count > 4:
            return lax.psum_scatter(
                parts, "dp", scatter_dimension=0, axis_index_groups=self.groups()
            ).astype(FULL)
        others = [
            self.swap(pick(parts, self.line ^ away, 0), away * self.stride)
            for away in range(1, count)
        ]
        return sum([other.astype(FULL) for other in others], pick(parts, self.line, 0).astype(FULL))

    def gather_rows(self, array):
        array = ordered(array, self.swap(array, self.row_mask), self.row, 0)
        array = ordered(array, self.swap(array, self.core_mask), self.core, 1)
        return array.reshape((-1,) + array.shape[3:])

    def gather_group(self, array):
        row, pair, both = [
            self.swap(array, mask)
            for mask in (self.row_mask, self.pair_mask, self.row_mask | self.pair_mask)
        ]
        array = ordered(
            ordered(array, row, self.row, 0), ordered(pair, both, self.row, 0), self.pair, 0
        )
        array = ordered(array, self.swap(array, self.core_mask), self.core, 2)
        return array.reshape((-1,) + array.shape[4:])

    def halve(self, array, mask, bit, axis):
        other = self.swap(pick(array, 1 - bit, axis).astype(LOW), mask)
        return pick(array, bit, axis).astype(FULL) + other.astype(FULL)

    def scatter_rows(self, array):
        array = array.reshape((2, 2, -1) + array.shape[1:])
        array = self.halve(array, self.core_mask, self.core, 1)
        return self.halve(array, self.row_mask, self.row, 0)

    def scatter_group(self, array):
        array = array.reshape((2, 2, 2, -1) + array.shape[1:])
        array = self.halve(array, self.core_mask, self.core, 2).astype(LOW)

        def part(pair, row):
            return pick(pick(array, pair, 0), row, 0)

        others = [
            self.swap(part(1 - self.pair, 1 - self.row), self.pair_mask | self.row_mask),
            self.swap(part(1 - self.pair, self.row), self.pair_mask),
            self.swap(part(self.pair, 1 - self.row), self.row_mask),
        ]
        return sum([other.astype(FULL) for other in others], part(self.pair, self.row).astype(FULL))

    def sum_all(self, array):
        mask = 1
        while mask < self.devices:
            array = array + self.swap(array, mask)
            mask *= 2
        return array


def wide_of(columns):
    half = columns // 2
    return -(-half // LANES) * LANES


def channel_part(weight, owner):
    columns = weight.shape[1]
    half, wide = columns // 2, wide_of(columns)
    offset = columns - wide
    window = jnp.where(owner == 0, weight[:, :wide], weight[:, offset:])
    place = lax.broadcasted_iota(jnp.int32, window.shape, 1) + jnp.where(owner == 0, 0, offset)
    return jnp.where((place < half) == (owner == 0), window, jnp.zeros_like(window))


def spread_channels(plan, weights):
    mine, theirs = [
        jnp.concatenate([channel_part(weight, owner) for weight in weights], axis=1)
        for owner in (plan.pair, 1 - plan.pair)
    ]
    both = ordered(mine, plan.swap(theirs, plan.pair_mask), plan.pair, 0)
    return both.reshape((-1, both.shape[-1]))


def collect_channels(plan, summed, columns):
    wide = wide_of(columns)
    summed = summed.reshape((2, -1, summed.shape[1]))
    other = plan.swap(pick(summed, 1 - plan.pair, 0), plan.pair_mask).astype(FULL)
    mine = pick(summed, plan.pair, 0).astype(FULL)
    first = jnp.where(plan.pair == 0, mine, other)
    second = jnp.where(plan.pair == 0, other, mine)
    offset = columns - wide
    results = []
    for start in range(0, summed.shape[2], wide):
        low, high = first[:, start : start + wide], second[:, start : start + wide]
        results.append(
            jnp.concatenate(
                [
                    low[:, :offset],
                    low[:, offset:] + high[:, : wide - offset],
                    high[:, wide - offset :],
                ],
                axis=1,
            )
        )
    return results


def gather_model(plan, weight):
    lines = plan.gather_lines_direct(weight)
    both = ordered(lines, plan.swap(lines, plan.pair_mask), plan.pair, 1)
    return both.reshape((-1, both.shape[-1]))


def scatter_model(plan, grad):
    grad = grad.astype(LOW).reshape((plan.lines, 2, -1, grad.shape[1]))
    grad = plan.halve(grad, plan.pair_mask, plan.pair, 1).astype(LOW)
    return plan.sum_lines_direct(grad)


def body(
    plan,
    tokens,
    segment_ids,
    positions,
    norm_in_gain,
    w_query,
    w_key,
    w_value,
    query_gain,
    key_gain,
    w_output,
    norm_mid_gain,
    w_gate,
    w_up,
    w_down,
    grad_out,
):
    plan.here()
    head_dim = query_gain.shape[0]
    scaling = head_dim ** (-0.5)
    sequences, length = segment_ids.shape
    rows = sequences * length
    q_columns, k_columns = w_query.shape[1], w_key.shape[1]
    heads = q_columns // head_dim
    groups = k_columns // head_dim
    repeat = heads // groups
    channels = w_gate.shape[1]

    qkv_columns = q_columns + 2 * k_columns
    wide = wide_of(channels)

    model_full = gather_model(
        plan, jnp.concatenate([w_query, w_key, w_value, w_output.T], axis=1)
    )
    qkv_full = model_full[:, :qkv_columns]
    output_own = model_full[:, qkv_columns:]
    tokens_seq = plan.gather_rows(tokens)
    windows = spread_channels(plan, [w_gate, w_up, w_down.T])
    gate_up_full = plan.gather_lines(windows[:, : 2 * wide])
    down_full = plan.gather_lines(windows[:, 2 * wide :])
    back_group = plan.gather_group(grad_out)

    inputs = tokens_seq.astype(FULL)
    scaled_in = inputs * scale_of(inputs)
    rows_in = (scaled_in * norm_in_gain).astype(LOW)
    qkv = matmul(rows_in, qkv_full)
    query_raw = qkv[:, :q_columns]
    key_raw = qkv[:, q_columns : q_columns + k_columns]
    value_low = qkv[:, q_columns + k_columns :].astype(LOW)
    cosine, sine = angles_of(positions.reshape(rows), head_dim)

    def heads_local(query_in, key_in, query_scale, key_scale):
        query_out = rotate(
            normalize(query_in.reshape(rows, heads, head_dim), query_scale), cosine, sine
        )
        key_out = rotate(normalize(key_in.reshape(rows, groups, head_dim), key_scale), cosine, sine)
        return (query_out, key_out)

    (query_rot, key_rot), pull_heads = jax.vjp(
        heads_local, query_raw, key_raw, query_gain, key_gain
    )
    query_low = query_rot.astype(LOW).reshape(sequences, length, groups, repeat, head_dim)
    key_low = key_rot.astype(LOW).reshape(sequences, length, groups, head_dim)
    value_seq = value_low.reshape(sequences, length, groups, head_dim)

    def forward_one(query, key, value, segment):
        scores = (
            jnp.einsum("qgrd,kgd->grqk", query, key, preferred_element_type=FULL) * scaling
        )
        index = jnp.arange(length)
        allowed = (segment[:, None] == segment[None, :]) & (index[None, :] <= index[:, None])
        scores = jnp.where(allowed, scores, -1e30)
        weights = jnp.exp(scores - jnp.max(scores, axis=-1, keepdims=True))
        probs = weights / jnp.sum(weights, axis=-1, keepdims=True)
        result = jnp.einsum("grqk,kgd->qgrd", probs.astype(LOW), value, preferred_element_type=FULL)
        return (result, probs)

    attended, probs_all = jax.vmap(forward_one)(query_low, key_low, value_seq, segment_ids)
    attended_low = attended.reshape(rows, heads * head_dim).astype(LOW)
    attn_part = plan.scatter_rows(matmul_back(attended_low, output_own).astype(LOW))

    middle = tokens.astype(FULL) + attn_part
    scaled_mid = middle * scale_of(middle)
    rows_mid = plan.gather_group((scaled_mid * norm_mid_gain).astype(LOW))
    gate_up = matmul(rows_mid, gate_up_full)
    gate_value, up_value = gate_up[:, :wide], gate_up[:, wide:]
    logistic = jax.nn.sigmoid(gate_value)
    swish = gate_value * logistic
    hidden_low = (swish * up_value).astype(LOW)
    down_sum = plan.sum_lines(matmul_rows(back_group, hidden_low).astype(LOW))
    grad_hidden = matmul(back_group, down_full)
    grad_gate_low = (
        grad_hidden * up_value * logistic * (1.0 + gate_value * (1.0 - logistic))
    ).astype(LOW)
    grad_up_low = (grad_hidden * swish).astype(LOW)
    grad_gate_up = jnp.concatenate([grad_gate_low, grad_up_low], axis=1)
    grad_normed_mid = plan.scatter_group(matmul_back(grad_gate_up, gate_up_full).astype(LOW))
    gain_mid = jnp.sum(grad_normed_mid * scaled_mid, axis=0)
    upstream = grad_out.astype(FULL)
    grad_middle = upstream + normalize_back(middle, norm_mid_gain, grad_normed_mid)
    rows_attn_back = plan.gather_rows(grad_middle.astype(LOW))

    gate_up_sum = plan.sum_lines(matmul_rows(rows_mid, grad_gate_up).astype(LOW))
    mlp_part = plan.scatter_group(matmul_back(hidden_low, down_full).astype(LOW))
    block_out = (middle + mlp_part).astype(LOW)
    (summed_down,) = collect_channels(plan, down_sum, channels)
    summed_gate, summed_up = collect_channels(plan, gate_up_sum, channels)

    grad_attended = matmul(rows_attn_back, output_own).astype(LOW)
    summed_output = scatter_model(plan, matmul_rows(rows_attn_back, attended_low)).T

    def backward_one(query, key, value, probs, grad_result):
        grad_probs = jnp.einsum("qgrd,kgd->grqk", grad_result, value, preferred_element_type=FULL)
        inner = jnp.sum(probs * grad_probs, axis=-1, keepdims=True)
        grad_scores = (probs * (grad_probs - inner)).astype(LOW)
        grad_query = (
            jnp.einsum("grqk,kgd->qgrd", grad_scores, key, preferred_element_type=FULL) * scaling
        )
        grad_key = (
            jnp.einsum("grqk,qgrd->kgd", grad_scores, query, preferred_element_type=FULL) * scaling
        )
        grad_value = jnp.einsum(
            "grqk,qgrd->kgd", probs.astype(LOW), grad_result, preferred_element_type=FULL
        )
        return (grad_query, grad_key, grad_value)

    grad_heads = grad_attended.reshape(sequences, length, groups, repeat, head_dim)
    grad_query_all, grad_key_all, grad_value_all = jax.vmap(backward_one)(
        query_low, key_low, value_seq, probs_all, grad_heads
    )
    grad_query_raw, grad_key_raw, grad_query_scale, grad_key_scale = pull_heads(
        (
            grad_query_all.reshape(rows, heads, head_dim),
            grad_key_all.reshape(rows, groups, head_dim),
        )
    )
    grad_qkv = jnp.concatenate(
        [
            grad_query_raw.astype(LOW),
            grad_key_raw.astype(LOW),
            grad_value_all.reshape(rows, k_columns).astype(LOW),
        ],
        axis=1,
    )
    summed_model = scatter_model(plan, matmul_rows(rows_in, grad_qkv))
    in_part = matmul_back(grad_qkv, qkv_full)
    gain_in = jnp.sum(in_part * scaled_in, axis=0)
    grad_normed_in = plan.scatter_rows(in_part.astype(LOW))
    grad_tokens = (
        grad_middle + normalize_back(tokens.astype(FULL), norm_in_gain, grad_normed_in)
    ).astype(LOW)

    gains = plan.sum_all(
        jnp.concatenate([gain_in, gain_mid, grad_query_scale, grad_key_scale])
    )
    width = gain_in.shape[0]
    return (
        block_out,
        grad_tokens,
        gains[:width],
        summed_model[:, :q_columns],
        summed_model[:, q_columns : q_columns + k_columns],
        summed_model[:, q_columns + k_columns :],
        gains[2 * width : 2 * width + head_dim],
        gains[2 * width + head_dim :],
        summed_output,
        gains[width : 2 * width],
        summed_gate,
        summed_up,
        summed_down.T,
    )


def solution(mesh):
    plan = Plan(mesh)

    def step(*args):
        return body(plan, *args)

    return jax.shard_map(
        step,
        mesh=mesh,
        in_specs=(
            P(("dp", "tensor"), None),
            P("dp", None),
            P("dp", None),
            P(),
            P("dp", "tensor"),
            P("dp", "tensor"),
            P("dp", "tensor"),
            P(),
            P(),
            P("tensor", "dp"),
            P(),
            P("dp", "tensor"),
            P("dp", "tensor"),
            P("tensor", "dp"),
            P(("dp", "tensor"), None),
        ),
        out_specs=(
            P(("dp", "tensor"), None),
            P(("dp", "tensor"), None),
            P(),
            P("dp", "tensor"),
            P("dp", "tensor"),
            P("dp", "tensor"),
            P(),
            P(),
            P("tensor", "dp"),
            P(),
            P("dp", "tensor"),
            P("dp", "tensor"),
            P("tensor", "dp"),
        ),
        check_vma=False,
    )
```

profile of v0, /device:TPU:0, one launch (start us, length us, event | category | flops | bytes accessed | tf_op | source)
XLA Modules:
  0.0 287.8 jit_solution(6455907070895421102)
XLA Ops:
  9.1 3.1 %collective-permute-start.2 = (bf16[128,768]{1,0:T(8,128)(2,1)S(1)}, bf16[128,768]{1,0:T(8,128)(2,1)}, u32[]{:S(2)}, u32[]{:S(2)}) collective-permute-start(bf16[128,768]{1,0:T(8,128)(2,1)S(1)} %pad_maximum_fusion.24), channel_id=1, source_target_pairs={{0,8},{1,9},{2,10},{3,11},{4,12},{5,13},{6,14},{7,15},{8,0},{9,1},... | collective-permute-start | bytes 589832 | tf_op jit(solution)/shard_map/ppermute | solution.py:90
  12.2 2.6 collective-permute-start.3
  22.4 7.1 %collective-permute-done.3 = bf16[128,768]{1,0:T(8,128)(2,1)} collective-permute-done((bf16[128,768]{1,0:T(8,128)(2,1)S(1)}, bf16[128,768]{1,0:T(8,128)(2,1)}, u32[]{:S(2)}, u32[]{:S(2)}) %collective-permute-start.3) | collective-permute-done | bytes 196640 | tf_op jit(solution)/shard_map/ppermute | solution.py:90
  40.1 8.0 %collective-permute-done.5 = bf16[4,128,768]{2,1,0:T(8,128)(2,1)} collective-permute-done((bf16[4,128,768]{2,1,0:T(8,128)(2,1)S(1)}, bf16[4,128,768]{2,1,0:T(8,128)(2,1)}, u32[]{:S(2)}, u32[]{:S(2)}) %collective-permute-start.5) | collective-permute-done | bytes 786464 | tf_op jit(solution)/shard_map/ppermute | solution.py:90
  60.5 12.6 %collective-permute-done.17 = bf16[128,1024]{1,0:T(8,128)(2,1)} collective-permute-done((bf16[128,1024]{1,0:T(8,128)(2,1)S(1)}, bf16[128,1024]{1,0:T(8,128)(2,1)}, u32[]{:S(2)}, u32[]{:S(2)}) %collective-permute-start.17) | collective-permute-done | bytes 262176 | tf_op jit(solution)/shard_map/ppermute | solution.py:90
  82.7 8.3 %collective-permute-done.8 = bf16[128,1024]{1,0:T(8,128)(2,1)S(1)} collective-permute-done((bf16[128,1024]{1,0:T(8,128)(2,1)S(1)}, bf16[128,1024]{1,0:T(8,128)(2,1)S(1)}, u32[]{:S(2)}, u32[]{:S(2)}) %collective-permute-start.8) | collective-permute-done | bytes 262176 | tf_op jit(solution)/shard_map/ppermute | solution.py:90
  102.4 7.6 %fusion.79 = f32[1024,1280]{1,0:T(8,128)} fusion(bf16[1024,1024]{1,0:T(8,128)(2,1)} %bitcast.341, bf16[1024,1280]{1,0:T(8,128)(2,1)} %all-gather.3.cloned.1.call-done), kind=kOutput, calls=%fused_computation.241 | convolution fusion | flops 2684354560 | bytes 9961472 | tf_op jit(solution)/shard_map/dot_general | solution.py:14
  110.1 20.7 %all-gather.5.cloned.1.call-done = bf16[1024,640]{1,0:T(8,128)(2,1)} async-done(((bf16[256,640]{1,0:T(8,128)(2,1)}), bf16[1024,640]{1,0:T(8,128)(2,1)}) %all-gather.5.cloned.1.call-update) | async-done | bytes 1310736 | tf_op jit(solution)/shard_map/all_gather | solution.py:98
  130.8 7.3 %multiply_convert_fusion.1 = (bf16[1024,640]{1,0:T(8,128)(2,1)S(1)}, bf16[1024,640]{1,0:T(8,128)(2,1)S(1)}, bf16[1024,640]{1,0:T(8,128)(2,1)}) fusion(f32[1024,1280]{1,0:T(8,128)} %fusion.79, bf16[1024,1024]{1,0:T(8,128)(2,1)} %bitcast.343, bf16[1024,640]{1,0:T(8,128)(2,1)} %all-gather.5.cloned.1.call-done), kind=kOutput, calls=%fused_computation.13 | convolution fusion | flops 1352007680 | bytes 12582912 | tf_op jit(solution)/shard_map/dot_general | solution.py:14
  138.1 3.1 %convolution_convert_fusion.1 = bf16[1024,1024]{1,0:T(8,128)(2,1)S(1)} fusion(bf16[1024,1280]{1,0:T(8,128)(2,1)S(1)} %copy-done.68, bf16[1024,640]{1,0:T(8,128)(2,1)S(1)} %get-tuple-element.64, bf16[1024,640]{1,0:T(8,128)(2,1)S(1)} %get-tuple-element.63), kind=kOutput, calls=%fused_computation.32 | convolution fusion | flops 2690646016 | bytes 7340032 | tf_op jit(solution)/shard_map/dot_general | solution.py:18
  142.9 4.9 %convolution_convert_fusion.3 = bf16[1024,640]{1,0:T(8,128)(2,1)} fusion(bf16[1024,1024]{1,0:T(8,128)(2,1)} %bitcast.344, bf16[1024,640]{1,0:T(8,128)(2,1)} %get-tuple-element.65), kind=kOutput, calls=%fused_computation.34 | convolution fusion | flops 1342832640 | bytes 4718592 | tf_op jit(solution)/shard_map/dot_general | solution.py:22
  149.9 2.5 collective-permute-start.22
  153.5 6.6 %collective-permute-done.22 = bf16[128,1024]{1,0:T(8,128)(2,1)S(1)} collective-permute-done((bf16[128,1024]{1,0:T(8,128)(2,1)S(1)}, bf16[128,1024]{1,0:T(8,128)(2,1)S(1)}, u32[]{:S(2)}, u32[]{:S(2)}) %collective-permute-start.22) | collective-permute-done | bytes 262176 | tf_op jit(solution)/shard_map/ppermute | solution.py:90
  160.0 5.2 %collective-permute-done.23 = bf16[128,1024]{1,0:T(8,128)(2,1)S(1)} collective-permute-done((bf16[128,1024]{1,0:T(8,128)(2,1)S(1)}, bf16[128,1024]{1,0:T(8,128)(2,1)S(1)}, u32[]{:S(2)}, u32[]{:S(2)}) %collective-permute-start.23) | collective-permute-done | bytes 262176 | tf_op jit(solution)/shard_map/ppermute | solution.py:90
  169.8 4.8 %collective-permute-done.25 = bf16[128,1024]{1,0:T(8,128)(2,1)S(1)} collective-permute-done((bf16[128,1024]{1,0:T(8,128)(2,1)S(1)}, bf16[128,1024]{1,0:T(8,128)(2,1)S(1)}, u32[]{:S(2)}, u32[]{:S(2)}) %collective-permute-start.25) | collective-permute-done | bytes 262176 | tf_op jit(solution)/shard_map/ppermute | solution.py:90
  174.8 13.3 %convolution_convert_fusion = bf16[1024,1280]{1,0:T(8,128)(2,1)} fusion(bf16[1024,1024]{1,0:T(8,128)(2,1)S(1)} %bitcast.342, bf16[1024,640]{1,0:T(8,128)(2,1)S(1)} %copy-done.74, bf16[1024,640]{1,0:T(8,128)(2,1)S(1)} %copy-done.72), kind=kOutput, calls=%fused_computation.7 | convolution fusion | flops 2690908160 | bytes 7340032 | tf_op jit(solution)/shard_map/dot_general | solution.py:22
  209.1 3.1 %convolution_convert_fusion.5 = bf16[1024,512]{1,0:T(8,128)(2,1)} fusion(bf16[512,1024]{1,0:T(8,128)(2,1)} %copy-done.23, bf16[512,128]{0,1:T(8,128)(2,1)} %bitcast.376, bf16[512,128]{0,1:T(8,128)(2,1)S(1)} %bitcast.368, bf16[512,256]{0,1:T(8,128)(2,1)} %bitcast.364), kind=kOutput, calls=%fused_computation.37 | convolution fusion | flops 538968064 | bytes 2621440 | tf_op jit(solution)/shard_map/dot_general | solution.py:22
  213.4 2.5 collective-permute-done.30
  227.3 2.7 collective-permute-done.33
  231.8 2.5 collective-permute-start.40
  236.7 2.8 collective-permute-done.39
  240.9 2.5 collective-permute-done.40
  255.4 4.9 %collective-permute-done.36 = bf16[128,512]{1,0:T(8,128)(2,1)} collective-permute-done((bf16[128,512]{1,0:T(8,128)(2,1)}, bf16[128,512]{1,0:T(8,128)(2,1)}, u32[]{:S(2)}, u32[]{:S(2)}) %collective-permute-start.36) | collective-permute-done | bytes 131104 | tf_op jit(solution)/shard_map/ppermute | solution.py:90
  276.0 3.1 %collective-permute-done.42 = bf16[128,1280]{1,0:T(8,128)(2,1)S(1)} collective-permute-done((bf16[128,1280]{1,0:T(8,128)(2,1)S(1)}, bf16[128,1280]{1,0:T(8,128)(2,1)S(1)}, u32[]{:S(2)}, u32[]{:S(2)}) %collective-permute-start.42) | collective-permute-done | bytes 327712 | tf_op jit(solution)/shard_map/ppermute | solution.py:90
  (372 shorter events, 130.5 us)
Async XLA Ops:
  7.2 95.2 %all-gather.3.cloned.1.call-start = ((), (), s32[]{:S(2)}) async-start(), calls=%async_computation.2 | async-start | bytes 3276800 | tf_op jit(solution)/shard_map/all_gather | solution.py:98
  12.2 17.3 %collective-permute-start.3 = (bf16[128,768]{1,0:T(8,128)(2,1)S(1)}, bf16[128,768]{1,0:T(8,128)(2,1)}, u32[]{:S(2)}, u32[]{:S(2)}) collective-permute-start(bf16[128,768]{1,0:T(8,128)(2,1)S(1)} %pad_maximum_fusion.24), channel_id=1, source_target_pairs={{0,16},{1,17},{2,18},{3,19},{4,20},{5,21},{6,22},{7,23},{8,24},{9,... | collective-permute-start | bytes 589832 | tf_op jit(solution)/shard_map/ppermute | solution.py:90
  14.8 15.6 %collective-permute-start.4 = (bf16[128,768]{1,0:T(8,128)(2,1)S(1)}, bf16[128,768]{1,0:T(8,128)(2,1)S(1)}, u32[]{:S(2)}, u32[]{:S(2)}) collective-permute-start(bf16[128,768]{1,0:T(8,128)(2,1)S(1)} %pad_maximum_fusion.24), channel_id=1, source_target_pairs={{0,24},{1,25},{2,26},{3,27},{4,28},{5,29},{6,30},{7,31},{8,16},{9,... | collective-permute-start | bytes 589832 | tf_op jit(solution)/shard_map/ppermute | solution.py:90
  14.8 17.2 %collective-permute-start = (bf16[128,1024]{1,0:T(8,128)(2,1)}, bf16[128,1024]{1,0:T(8,128)(2,1)}, u32[]{:S(2)}, u32[]{:S(2)}) collective-permute-start(bf16[128,1024]{1,0:T(8,128)(2,1)} %param.15), channel_id=1, source_target_pairs={{0,2},{1,3},{2,0},{3,1},{4,6},{5,7},{6,4},{7,5},{8,10},{9,11},{10,... | collective-permute-start | bytes 786440 | tf_op jit(solution)/shard_map/ppermute | solution.py:90
  19.1 14.7 %collective-permute-start.12 = (bf16[128,1920]{1,0:T(8,128)(2,1)S(1)}, bf16[128,1920]{1,0:T(8,128)(2,1)S(1)}, u32[]{:S(2)}, u32[]{:S(2)}) collective-permute-start(bf16[128,1920]{1,0:T(8,128)(2,1)S(1)} %pad_maximum_fusion.20), channel_id=1, source_target_pairs={{0,4},{1,5},{2,6},{3,7},{4,0},{5,1},{6,2},{7,3},{8,12},{9,13},{10,... | collective-permute-start | bytes 1474568 | tf_op jit(solution)/shard_map/ppermute | solution.py:90
  30.5 17.6 %collective-permute-start.5 = (bf16[4,128,768]{2,1,0:T(8,128)(2,1)S(1)}, bf16[4,128,768]{2,1,0:T(8,128)(2,1)}, u32[]{:S(2)}, u32[]{:S(2)}) collective-permute-start(bf16[4,128,768]{2,1,0:T(8,128)(2,1)S(1)} %bitcast_dynamic-update-slice_fusion), channel_id=1, source_target_pairs={{0,4},{1,5},{2,6},{3,7},{4,0},{5,1},{6,2},{7,3},{8,12},{9,13},{10,... | collective-permute-start | bytes 2359304 | tf_op jit(solution)/shard_map/ppermute | solution.py:90
  37.8 93.0 %all-gather.5.cloned.1.call-start = ((), (), s32[]{:S(2)}) async-start(), calls=%async_computation.3 | async-start | bytes 1638400 | tf_op jit(solution)/shard_map/all_gather | solution.py:98
  56.1 17.9 %collective-permute-start.18 = (bf16[128,1024]{1,0:T(8,128)(2,1)S(1)}, bf16[128,1024]{1,0:T(8,128)(2,1)}, u32[]{:S(2)}, u32[]{:S(2)}) collective-permute-start(bf16[128,1024]{1,0:T(8,128)(2,1)S(1)} %copy-done.14), channel_id=1, source_target_pairs={{0,4},{1,5},{2,6},{3,7},{4,0},{5,1},{6,2},{7,3},{8,12},{9,13},{10,... | collective-permute-start | bytes 786440 | tf_op jit(solution)/shard_map/ppermute | solution.py:90
  57.6 16.5 %collective-permute-start.19 = (bf16[128,1024]{1,0:T(8,128)(2,1)S(1)}, bf16[128,1024]{1,0:T(8,128)(2,1)}, u32[]{:S(2)}, u32[]{:S(2)}) collective-permute-start(bf16[128,1024]{1,0:T(8,128)(2,1)S(1)} %copy-done.14), channel_id=1, source_target_pairs={{0,6},{1,7},{2,4},{3,5},{4,2},{5,3},{6,0},{7,1},{8,14},{9,15},{10,... | collective-permute-start | bytes 786440 | tf_op jit(solution)/shard_map/ppermute | solution.py:90
  58.2 14.9 %collective-permute-start.17 = (bf16[128,1024]{1,0:T(8,128)(2,1)S(1)}, bf16[128,1024]{1,0:T(8,128)(2,1)}, u32[]{:S(2)}, u32[]{:S(2)}) collective-permute-start(bf16[128,1024]{1,0:T(8,128)(2,1)S(1)} %copy-done.14), channel_id=1, source_target_pairs={{0,2},{1,3},{2,0},{3,1},{4,6},{5,7},{6,4},{7,5},{8,10},{9,11},{10,... | collective-permute-start | bytes 786440 | tf_op jit(solution)/shard_map/ppermute | solution.py:90
  59.9 17.7 %collective-permute-start.7 = (bf16[128,1024]{1,0:T(8,128)(2,1)S(1)}, bf16[128,1024]{1,0:T(8,128)(2,1)S(1)}, u32[]{:S(2)}, u32[]{:S(2)}) collective-permute-start(bf16[128,1024]{1,0:T(8,128)(2,1)S(1)} %fusion.49), channel_id=1, source_target_pairs={{0,2},{1,3},{2,0},{3,1},{4,6},{5,7},{6,4},{7,5},{8,10},{9,11},{10,... | collective-permute-start | bytes 786440 | tf_op jit(solution)/shard_map/ppermute | solution.py:90
  77.9 13.1 %collective-permute-start.8 = (bf16[128,1024]{1,0:T(8,128)(2,1)S(1)}, bf16[128,1024]{1,0:T(8,128)(2,1)S(1)}, u32[]{:S(2)}, u32[]{:S(2)}) collective-permute-start(bf16[128,1024]{1,0:T(8,128)(2,1)S(1)} %multiply_convert_fusion.4), channel_id=1, source_target_pairs={{0,2},{1,3},{2,0},{3,1},{4,6},{5,7},{6,4},{7,5},{8,10},{9,11},{10,... | collective-permute-start | bytes 786440 | tf_op jit(solution)/shard_map/ppermute | solution.py:90
  82.7 13.8 %collective-permute-start.20 = (bf16[2,2,128,1024]{3,2,1,0:T(8,128)(2,1)}, bf16[2,2,128,1024]{3,2,1,0:T(8,128)(2,1)}, u32[]{:S(2)}, u32[]{:S(2)}) collective-permute-start(bf16[2,2,128,1024]{3,2,1,0:T(8,128)(2,1)} %pad_maximum_fusion.7), channel_id=1, source_target_pairs={{0,1},{1,0},{2,3},{3,2},{4,5},{5,4},{6,7},{7,6},{8,9},{9,8},{10,11... | collective-permute-start | bytes 3145736 | tf_op jit(solution)/shard_map/ppermute | solution.py:90
  96.2 154.6 %reduce-scatter.5.cloned.1.call-start = ((), (), s32[]{:S(2)}) async-start(), calls=%async_computation.5 | async-start | bytes 1638400 | tf_op jit(solution)/shard_map/reduce_scatter | solution.py:101
  147.8 123.1 %reduce-scatter.3.cloned.1.call-start = ((), (), s32[]{:S(2)}) async-start(), calls=%async_computation.4 | async-start | bytes 3276800 | tf_op jit(solution)/shard_map/reduce_scatter | solution.py:101
  152.4 12.9 %collective-permute-start.23 = (bf16[128,1024]{1,0:T(8,128)(2,1)S(1)}, bf16[128,1024]{1,0:T(8,128)(2,1)S(1)}, u32[]{:S(2)}, u32[]{:S(2)}) collective-permute-start(bf16[128,1024]{1,0:T(8,128)(2,1)S(1)} %get-tuple-element.80), channel_id=1, source_target_pairs={{0,4},{1,5},{2,6},{3,7},{4,0},{5,1},{6,2},{7,3},{8,12},{9,13},{10,... | collective-permute-start | bytes 786440 | tf_op jit(solution)/shard_map/ppermute | solution.py:90
  169.7 18.5 %collective-permute-start.13 = (bf16[2,2,128,1024]{3,2,1,0:T(8,128)(2,1)S(1)}, bf16[2,2,128,1024]{3,2,1,0:T(8,128)(2,1)}, u32[]{:S(2)}, u32[]{:S(2)}) collective-permute-start(bf16[2,2,128,1024]{3,2,1,0:T(8,128)(2,1)S(1)} %dynamic-slice_bitcast_fusion.1), channel_id=1, source_target_pairs={{0,1},{1,0},{2,3},{3,2},{4,5},{5,4},{6,7},{7,6},{8,9},{9,8},{10,11... | collective-permute-start | bytes 3145736 | tf_op jit(solution)/shard_map/ppermute | solution.py:90
  174.7 18.8 %collective-permute-start.26 = (bf16[2,128,1024]{2,1,0:T(8,128)(2,1)S(1)}, bf16[2,128,1024]{2,1,0:T(8,128)(2,1)}, u32[]{:S(2)}, u32[]{:S(2)}) collective-permute-start(bf16[2,128,1024]{2,1,0:T(8,128)(2,1)S(1)} %pad_maximum_fusion.17), channel_id=1, source_target_pairs={{0,1},{1,0},{2,3},{3,2},{4,5},{5,4},{6,7},{7,6},{8,9},{9,8},{10,11... | collective-permute-start | bytes 1572872 | tf_op jit(solution)/shard_map/ppermute | solution.py:90
  191.1 82.4 %collective-permute-start.14 = (bf16[128,1024]{1,0:T(8,128)(2,1)}, bf16[128,1024]{1,0:T(8,128)(2,1)}, u32[]{:S(2)}, u32[]{:S(2)}) collective-permute-start(bf16[128,1024]{1,0:T(8,128)(2,1)} %get-tuple-element.83), channel_id=1, source_target_pairs={{0,6},{1,7},{2,4},{3,5},{4,2},{5,3},{6,0},{7,1},{8,14},{9,15},{10,... | collective-permute-start | bytes 786440 | tf_op jit(solution)/shard_map/ppermute | solution.py:90
  217.4 13.2 %collective-permute-start.38 = (bf16[4,128,256]{1,2,0:T(8,128)(2,1)}, bf16[4,128,256]{1,2,0:T(8,128)(2,1)}, u32[]{:S(2)}, u32[]{:S(2)}) collective-permute-start(bf16[4,128,256]{1,2,0:T(8,128)(2,1)} %bitcast.118), channel_id=1, source_target_pairs={{0,4},{1,5},{2,6},{3,7},{4,0},{5,1},{6,2},{7,3},{8,12},{9,13},{10,... | collective-permute-start | bytes 786440 | tf_op jit(solution)/shard_map/ppermute | solution.py:90
  222.3 21.8 %collective-permute-start.34 = (bf16[4,128,512]{2,1,0:T(8,128)(2,1)}, bf16[4,128,512]{2,1,0:T(8,128)(2,1)S(1)}, u32[]{:S(2)}, u32[]{:S(2)}) collective-permute-start(bf16[4,128,512]{2,1,0:T(8,128)(2,1)} %dynamic-slice_bitcast_fusion.2), channel_id=1, source_target_pairs={{0,4},{1,5},{2,6},{3,7},{4,0},{5,1},{6,2},{7,3},{8,12},{9,13},{10,... | collective-permute-start | bytes 1572872 | tf_op jit(solution)/shard_map/ppermute | solution.py:90
  239.5 34.0 %collective-permute-start.15 = (bf16[128,1024]{1,0:T(8,128)(2,1)}, bf16[128,1024]{1,0:T(8,128)(2,1)}, u32[]{:S(2)}, u32[]{:S(2)}) collective-permute-start(bf16[128,1024]{1,0:T(8,128)(2,1)} %get-tuple-element.85), channel_id=1, source_target_pairs={{0,4},{1,5},{2,6},{3,7},{4,0},{5,1},{6,2},{7,3},{8,12},{9,13},{10,... | collective-permute-start | bytes 786440 | tf_op jit(solution)/shard_map/ppermute | solution.py:90
  248.6 13.3 %collective-permute-start.37 = (bf16[128,512]{1,0:T(8,128)(2,1)}, bf16[128,512]{1,0:T(8,128)(2,1)}, u32[]{:S(2)}, u32[]{:S(2)}) collective-permute-start(bf16[128,512]{1,0:T(8,128)(2,1)} %get-tuple-element.105), channel_id=1, source_target_pairs={{0,24},{1,25},{2,26},{3,27},{4,28},{5,29},{6,30},{7,31},{8,16},{9,... | collective-permute-start | bytes 393224 | tf_op jit(solution)/shard_map/ppermute | solution.py:90
  253.9 19.7 %collective-permute-start.16 = (bf16[128,1024]{1,0:T(8,128)(2,1)}, bf16[128,1024]{1,0:T(8,128)(2,1)}, u32[]{:S(2)}, u32[]{:S(2)}) collective-permute-start(bf16[128,1024]{1,0:T(8,128)(2,1)} %get-tuple-element.84), channel_id=1, source_target_pairs={{0,2},{1,3},{2,0},{3,1},{4,6},{5,7},{6,4},{7,5},{8,10},{9,11},{10,... | collective-permute-start | bytes 786440 | tf_op jit(solution)/shard_map/ppermute | solution.py:90
  (102 other events, 737.5 us)
Sparse Core Ops, SparseCore 0:
  37.9 54.9 all-gather.2
  96.3 34.4 all-gather.4
  147.9 30.3 reduce-scatter.4
  188.3 55.8 reduce-scatter.2
where the time goes:
time: 292 us; the launch traced here: 288 us
  waiting for transfers between devices  99.5 us (34%)
  matrix products  51.8 us (18%)
  starting transfers between devices  47.5 us (16%)
  other arithmetic  40.9 us (14%)
  local copies, waits for them, and re-layouts  32.5 us (11%)
  between operations  15.6 us (5%)
    ppermute x44, waiting for transfers between devices, swap(): lax.ppermute(array, AXES, [(i, i ^ mask) for i in range(self.devices)])  78.7 us
    ppermute x44, starting transfers between devices, swap(): lax.ppermute(array, AXES, [(i, i ^ mask) for i in range(self.devices)])  47.1 us
    dot_general x4, matrix products, matmul_rows(): lax.dot_general(left, right, (((0,), (0,)), ((), ())), preferred_element_...  21.8 us
    all_gather x2, waiting for transfers between devices, gather_lines(): lax.all_gather(array, 'dp', axis=0, tiled=True, axis_index_groups=self.gr...  20.7 us
    dot_general x4, matrix products, matmul(): return jnp.dot(left, right, preferred_element_type=FULL)  16.2 us
    another operation x21, other arithmetic, ordered(): jnp.stack([jnp.where(first, mine, other), jnp.where(first, other, mine)],...  15.9 us
    unnamed x156, local copies, waits for them, and re-layouts  11.9 us
    squeeze x11, local copies, waits for them, and re-layouts, pick(): return lax.dynamic_index_in_dim(array, index, axis, keepdims=False)  8.57 us
  transfers between devices with their start and end apart: 48, of which 20 were waited for; matrix products, arithmetic and copies ran while one was open for 36% of the time, Pallas kernels for 0%

commit v1 on v0

--- a/solution.py
+++ b/solution.py
@@ -322,8 +322,9 @@
     logistic = jax.nn.sigmoid(gate_value)
     swish = gate_value * logistic
     hidden_low = (swish * up_value).astype(LOW)
-    down_sum = plan.sum_lines(matmul_rows(back_group, hidden_low).astype(LOW))
-    grad_hidden = matmul(back_group, down_full)
+    grad_down = matmul_rows(back_group, hidden_low).astype(LOW)
+    down_sum = plan.sum_lines(grad_down)
+    grad_hidden = matmul(back_group, after(down_full, grad_down))
     grad_gate_low = (
         grad_hidden * up_value * logistic * (1.0 + gate_value * (1.0 - logistic))
     ).astype(LOW)

time: 292 us -> 288 us (0.986)
  matrix products: 51.8 us -> 46.3 us
    all_gather x2, waiting for transfers between devices: 20.7 us -> 16.9 us  [gather_lines(): lax.all_gather(array, 'dp', axis=0, tiled=True, axis_index_groups=self.gr...]
    dot_general x4, matrix products: 16.2 us -> 12.6 us  [matmul(): return jnp.dot(left, right, preferred_element_type=FULL)]
    unnamed x156 -> x162, local copies, waits for them, and re-layouts: 11.9 us -> 14.3 us
  transfers between devices with their start and end apart: 48 -> 48, of which waited for: 20 -> 21; matrix products, arithmetic and copies ran while one was open for 36% -> 35% of each run, Pallas kernels for 0% -> 0%
where the time goes in v1:
time: 288 us; the launch traced here: 284 us
  waiting for transfers between devices  97.9 us (34%)
  starting transfers between devices  47.5 us (16%)
  matrix products  46.3 us (16%)
  other arithmetic  41.6 us (14%)
  local copies, waits for them, and re-layouts  35 us (12%)
  between operations  15.7 us (5%)
    ppermute x44, waiting for transfers between devices, swap(): lax.ppermute(array, AXES, [(i, i ^ mask) for i in range(self.devices)])  80.9 us
    ppermute x44, starting transfers between devices, swap(): lax.ppermute(array, AXES, [(i, i ^ mask) for i in range(self.devices)])  47.1 us
    dot_general x4, matrix products, matmul_rows(): lax.dot_general(left, right, (((0,), (0,)), ((), ())), preferred_element_...  19.9 us
    all_gather x2, waiting for transfers between devices, gather_lines(): lax.all_gather(array, 'dp', axis=0, tiled=True, axis_index_groups=self.gr...  16.9 us
    another operation x21, other arithmetic, ordered(): jnp.stack([jnp.where(first, mine, other), jnp.where(first, other, mine)],...  15.9 us
    unnamed x162, local copies, waits for them, and re-layouts  14.3 us
    dot_general x4, matrix products, matmul(): return jnp.dot(left, right, preferred_element_type=FULL)  12.6 us
    squeeze x11, local copies, waits for them, and re-layouts, pick(): return lax.dynamic_index_in_dim(array, index, axis, keepdims=False)  8.56 us
  transfers between devices with their start and end apart: 48, of which 21 were waited for; matrix products, arithmetic and copies ran while one was open for 35% of the time, Pallas kernels for 0%

profile of v1, /device:TPU:0, one launch (start us, length us, event | category | flops | bytes accessed | tf_op | source)
XLA Modules:
  0.0 284.0 jit_solution(18268031971941980346)
XLA Ops:
  9.1 3.1 %collective-permute-start.2 = (bf16[128,768]{1,0:T(8,128)(2,1)S(1)}, bf16[128,768]{1,0:T(8,128)(2,1)}, u32[]{:S(2)}, u32[]{:S(2)}) collective-permute-start(bf16[128,768]{1,0:T(8,128)(2,1)S(1)} %pad_maximum_fusion.24), channel_id=1, source_target_pairs={{0,8},{1,9},{2,10},{3,11},{4,12},{5,13},{6,14},{7,15},{8,0},{9,1},... | collective-permute-start | bytes 589832 | tf_op jit(solution)/shard_map/ppermute | solution.py:90
  12.2 2.6 collective-permute-start.3
  22.4 7.1 %collective-permute-done.3 = bf16[128,768]{1,0:T(8,128)(2,1)} collective-permute-done((bf16[128,768]{1,0:T(8,128)(2,1)S(1)}, bf16[128,768]{1,0:T(8,128)(2,1)}, u32[]{:S(2)}, u32[]{:S(2)}) %collective-permute-start.3) | collective-permute-done | bytes 196640 | tf_op jit(solution)/shard_map/ppermute | solution.py:90
  40.1 7.9 %collective-permute-done.5 = bf16[4,128,768]{2,1,0:T(8,128)(2,1)} collective-permute-done((bf16[4,128,768]{2,1,0:T(8,128)(2,1)S(1)}, bf16[4,128,768]{2,1,0:T(8,128)(2,1)}, u32[]{:S(2)}, u32[]{:S(2)}) %collective-permute-start.5) | collective-permute-done | bytes 786464 | tf_op jit(solution)/shard_map/ppermute | solution.py:90
  60.5 12.6 %collective-permute-done.17 = bf16[128,1024]{1,0:T(8,128)(2,1)} collective-permute-done((bf16[128,1024]{1,0:T(8,128)(2,1)S(1)}, bf16[128,1024]{1,0:T(8,128)(2,1)}, u32[]{:S(2)}, u32[]{:S(2)}) %collective-permute-start.17) | collective-permute-done | bytes 262176 | tf_op jit(solution)/shard_map/ppermute | solution.py:90
  82.7 8.3 %collective-permute-done.8 = bf16[128,1024]{1,0:T(8,128)(2,1)S(1)} collective-permute-done((bf16[128,1024]{1,0:T(8,128)(2,1)S(1)}, bf16[128,1024]{1,0:T(8,128)(2,1)S(1)}, u32[]{:S(2)}, u32[]{:S(2)}) %collective-permute-start.8) | collective-permute-done | bytes 262176 | tf_op jit(solution)/shard_map/ppermute | solution.py:90
  102.4 5.3 %fusion.79 = f32[1024,1280]{1,0:T(8,128)S(1)} fusion(bf16[1024,1024]{1,0:T(8,128)(2,1)} %bitcast.341, bf16[1024,1280]{1,0:T(8,128)(2,1)} %all-gather.3.cloned.1.call-done), kind=kOutput, calls=%fused_computation.241 | convolution fusion | flops 2684354560 | bytes 9961472 | tf_op jit(solution)/shard_map/dot_general | solution.py:14
  110.9 3.0 %convolution_convert_fusion.3 = bf16[1024,640]{1,0:T(8,128)(2,1)} fusion(bf16[1024,1024]{1,0:T(8,128)(2,1)S(1)} %bitcast.344, bf16[1024,640]{1,0:T(8,128)(2,1)S(1)} %multiply_convert_fusion.2), kind=kOutput, calls=%fused_computation.34 | convolution fusion | flops 1342832640 | bytes 4718592 | tf_op jit(solution)/shard_map/dot_general | solution.py:22
  113.9 16.9 %all-gather.5.cloned.1.call-done = bf16[1024,640]{1,0:T(8,128)(2,1)} async-done(((bf16[256,640]{1,0:T(8,128)(2,1)}), bf16[1024,640]{1,0:T(8,128)(2,1)}) %all-gather.5.cloned.1.call-update) | async-done | bytes 1310736 | tf_op jit(solution)/shard_map/all_gather | solution.py:98
  130.8 6.0 %multiply_convert_fusion.1 = (bf16[1024,640]{1,0:T(8,128)(2,1)S(1)}, bf16[1024,640]{1,0:T(8,128)(2,1)S(1)}) fusion(f32[1024,1280]{1,0:T(8,128)} %copy-done.6, bf16[1024,1024]{1,0:T(8,128)(2,1)} %bitcast.343, bf16[1024,640]{1,0:T(8,128)(2,1)} %all-gather.5.cloned.1.call-done), kind=kOutput, calls=%fused_computation.13 | convolution fusion | flops 1350696960 | bytes 11272192 | tf_op jit(solution)/shard_map/dot_general | solution.py:14
  136.8 3.1 %convolution_convert_fusion.1 = bf16[1024,1024]{1,0:T(8,128)(2,1)S(1)} fusion(bf16[1024,1280]{1,0:T(8,128)(2,1)S(1)} %copy-done.72, bf16[1024,640]{1,0:T(8,128)(2,1)S(1)} %get-tuple-element.66, bf16[1024,640]{1,0:T(8,128)(2,1)S(1)} %get-tuple-element.65), kind=kOutput, calls=%fused_computation.32 | convolution fusion | flops 2690646016 | bytes 7340032 | tf_op jit(solution)/shard_map/dot_general | solution.py:18
  141.7 2.7 collective-permute-done.21
  150.0 6.6 %collective-permute-done.22 = bf16[128,1024]{1,0:T(8,128)(2,1)S(1)} collective-permute-done((bf16[128,1024]{1,0:T(8,128)(2,1)S(1)}, bf16[128,1024]{1,0:T(8,128)(2,1)S(1)}, u32[]{:S(2)}, u32[]{:S(2)}) %collective-permute-start.22) | collective-permute-done | bytes 262176 | tf_op jit(solution)/shard_map/ppermute | solution.py:90
  156.6 4.8 %collective-permute-done.23 = bf16[128,1024]{1,0:T(8,128)(2,1)S(1)} collective-permute-done((bf16[128,1024]{1,0:T(8,128)(2,1)S(1)}, bf16[128,1024]{1,0:T(8,128)(2,1)S(1)}, u32[]{:S(2)}, u32[]{:S(2)}) %collective-permute-start.23) | collective-permute-done | bytes 262176 | tf_op jit(solution)/shard_map/ppermute | solution.py:90
  166.0 4.8 %collective-permute-done.25 = bf16[128,1024]{1,0:T(8,128)(2,1)S(1)} collective-permute-done((bf16[128,1024]{1,0:T(8,128)(2,1)S(1)}, bf16[128,1024]{1,0:T(8,128)(2,1)S(1)}, u32[]{:S(2)}, u32[]{:S(2)}) %collective-permute-start.25) | collective-permute-done | bytes 262176 | tf_op jit(solution)/shard_map/ppermute | solution.py:90
  171.0 13.3 %convolution_convert_fusion = bf16[1024,1280]{1,0:T(8,128)(2,1)} fusion(bf16[1024,1024]{1,0:T(8,128)(2,1)S(1)} %bitcast.342, bf16[1024,640]{1,0:T(8,128)(2,1)S(1)} %copy-done.78, bf16[1024,640]{1,0:T(8,128)(2,1)S(1)} %copy-done.76), kind=kOutput, calls=%fused_computation.7 | convolution fusion | flops 2690908160 | bytes 7340032 | tf_op jit(solution)/shard_map/dot_general | solution.py:22
  205.2 3.1 %convolution_convert_fusion.5 = bf16[1024,512]{1,0:T(8,128)(2,1)} fusion(bf16[512,1024]{1,0:T(8,128)(2,1)} %copy-done.27, bf16[512,128]{0,1:T(8,128)(2,1)} %bitcast.376, bf16[512,128]{0,1:T(8,128)(2,1)S(1)} %bitcast.368, bf16[512,256]{0,1:T(8,128)(2,1)} %bitcast.364), kind=kOutput, calls=%fused_computation.37 | convolution fusion | flops 538968064 | bytes 2621440 | tf_op jit(solution)/shard_map/dot_general | solution.py:22
  209.6 2.5 collective-permute-done.30
  223.5 2.7 collective-permute-done.33
  227.9 2.5 collective-permute-start.40
  232.9 2.8 collective-permute-done.39
  237.1 2.5 collective-permute-done.40
  251.5 5.0 %collective-permute-done.36 = bf16[128,512]{1,0:T(8,128)(2,1)} collective-permute-done((bf16[128,512]{1,0:T(8,128)(2,1)}, bf16[128,512]{1,0:T(8,128)(2,1)}, u32[]{:S(2)}, u32[]{:S(2)}) %collective-permute-start.36) | collective-permute-done | bytes 131104 | tf_op jit(solution)/shard_map/ppermute | solution.py:90
  272.2 3.1 %collective-permute-done.42 = bf16[128,1280]{1,0:T(8,128)(2,1)S(1)} collective-permute-done((bf16[128,1280]{1,0:T(8,128)(2,1)S(1)}, bf16[128,1280]{1,0:T(8,128)(2,1)S(1)}, u32[]{:S(2)}, u32[]{:S(2)}) %collective-permute-start.42) | collective-permute-done | bytes 327712 | tf_op jit(solution)/shard_map/ppermute | solution.py:90
  (379 shorter events, 136.1 us)
Async XLA Ops:
  7.2 95.2 %all-gather.3.cloned.1.call-start = ((), (), s32[]{:S(2)}) async-start(), calls=%async_computation.2 | async-start | bytes 3276800 | tf_op jit(solution)/shard_map/all_gather | solution.py:98
  12.2 17.3 %collective-permute-start.3 = (bf16[128,768]{1,0:T(8,128)(2,1)S(1)}, bf16[128,768]{1,0:T(8,128)(2,1)}, u32[]{:S(2)}, u32[]{:S(2)}) collective-permute-start(bf16[128,768]{1,0:T(8,128)(2,1)S(1)} %pad_maximum_fusion.24), channel_id=1, source_target_pairs={{0,16},{1,17},{2,18},{3,19},{4,20},{5,21},{6,22},{7,23},{8,24},{9,... | collective-permute-start | bytes 589832 | tf_op jit(solution)/shard_map/ppermute | solution.py:90
  14.8 15.6 %collective-permute-start.4 = (bf16[128,768]{1,0:T(8,128)(2,1)S(1)}, bf16[128,768]{1,0:T(8,128)(2,1)S(1)}, u32[]{:S(2)}, u32[]{:S(2)}) collective-permute-start(bf16[128,768]{1,0:T(8,128)(2,1)S(1)} %pad_maximum_fusion.24), channel_id=1, source_target_pairs={{0,24},{1,25},{2,26},{3,27},{4,28},{5,29},{6,30},{7,31},{8,16},{9,... | collective-permute-start | bytes 589832 | tf_op jit(solution)/shard_map/ppermute | solution.py:90
  14.8 17.2 %collective-permute-start = (bf16[128,1024]{1,0:T(8,128)(2,1)}, bf16[128,1024]{1,0:T(8,128)(2,1)}, u32[]{:S(2)}, u32[]{:S(2)}) collective-permute-start(bf16[128,1024]{1,0:T(8,128)(2,1)} %param.15), channel_id=1, source_target_pairs={{0,2},{1,3},{2,0},{3,1},{4,6},{5,7},{6,4},{7,5},{8,10},{9,11},{10,... | collective-permute-start | bytes 786440 | tf_op jit(solution)/shard_map/ppermute | solution.py:90
  19.1 14.7 %collective-permute-start.12 = (bf16[128,1920]{1,0:T(8,128)(2,1)S(1)}, bf16[128,1920]{1,0:T(8,128)(2,1)S(1)}, u32[]{:S(2)}, u32[]{:S(2)}) collective-permute-start(bf16[128,1920]{1,0:T(8,128)(2,1)S(1)} %pad_maximum_fusion.20), channel_id=1, source_target_pairs={{0,4},{1,5},{2,6},{3,7},{4,0},{5,1},{6,2},{7,3},{8,12},{9,13},{10,... | collective-permute-start | bytes 1474568 | tf_op jit(solution)/shard_map/ppermute | solution.py:90
  30.5 17.6 %collective-permute-start.5 = (bf16[4,128,768]{2,1,0:T(8,128)(2,1)S(1)}, bf16[4,128,768]{2,1,0:T(8,128)(2,1)}, u32[]{:S(2)}, u32[]{:S(2)}) collective-permute-start(bf16[4,128,768]{2,1,0:T(8,128)(2,1)S(1)} %bitcast_dynamic-update-slice_fusion), channel_id=1, source_target_pairs={{0,4},{1,5},{2,6},{3,7},{4,0},{5,1},{6,2},{7,3},{8,12},{9,13},{10,... | collective-permute-start | bytes 2359304 | tf_op jit(solution)/shard_map/ppermute | solution.py:90
  37.9 92.9 %all-gather.5.cloned.1.call-start = ((), (), s32[]{:S(2)}) async-start(), calls=%async_computation.3 | async-start | bytes 1638400 | tf_op jit(solution)/shard_map/all_gather | solution.py:98
  56.1 17.9 %collective-permute-start.18 = (bf16[128,1024]{1,0:T(8,128)(2,1)S(1)}, bf16[128,1024]{1,0:T(8,128)(2,1)}, u32[]{:S(2)}, u32[]{:S(2)}) collective-permute-start(bf16[128,1024]{1,0:T(8,128)(2,1)S(1)} %copy-done.15), channel_id=1, source_target_pairs={{0,4},{1,5},{2,6},{3,7},{4,0},{5,1},{6,2},{7,3},{8,12},{9,13},{10,... | collective-permute-start | bytes 786440 | tf_op jit(solution)/shard_map/ppermute | solution.py:90
  57.6 16.5 %collective-permute-start.19 = (bf16[128,1024]{1,0:T(8,128)(2,1)S(1)}, bf16[128,1024]{1,0:T(8,128)(2,1)}, u32[]{:S(2)}, u32[]{:S(2)}) collective-permute-start(bf16[128,1024]{1,0:T(8,128)(2,1)S(1)} %copy-done.15), channel_id=1, source_target_pairs={{0,6},{1,7},{2,4},{3,5},{4,2},{5,3},{6,0},{7,1},{8,14},{9,15},{10,... | collective-permute-start | bytes 786440 | tf_op jit(solution)/shard_map/ppermute | solution.py:90
  58.1 14.9 %collective-permute-start.17 = (bf16[128,1024]{1,0:T(8,128)(2,1)S(1)}, bf16[128,1024]{1,0:T(8,128)(2,1)}, u32[]{:S(2)}, u32[]{:S(2)}) collective-permute-start(bf16[128,1024]{1,0:T(8,128)(2,1)S(1)} %copy-done.15), channel_id=1, source_target_pairs={{0,2},{1,3},{2,0},{3,1},{4,6},{5,7},{6,4},{7,5},{8,10},{9,11},{10,... | collective-permute-start | bytes 786440 | tf_op jit(solution)/shard_map/ppermute | solution.py:90
  59.9 17.7 %collective-permute-start.7 = (bf16[128,1024]{1,0:T(8,128)(2,1)S(1)}, bf16[128,1024]{1,0:T(8,128)(2,1)S(1)}, u32[]{:S(2)}, u32[]{:S(2)}) collective-permute-start(bf16[128,1024]{1,0:T(8,128)(2,1)S(1)} %fusion.49), channel_id=1, source_target_pairs={{0,2},{1,3},{2,0},{3,1},{4,6},{5,7},{6,4},{7,5},{8,10},{9,11},{10,... | collective-permute-start | bytes 786440 | tf_op jit(solution)/shard_map/ppermute | solution.py:90
  77.9 13.1 %collective-permute-start.8 = (bf16[128,1024]{1,0:T(8,128)(2,1)S(1)}, bf16[128,1024]{1,0:T(8,128)(2,1)S(1)}, u32[]{:S(2)}, u32[]{:S(2)}) collective-permute-start(bf16[128,1024]{1,0:T(8,128)(2,1)S(1)} %multiply_convert_fusion.4), channel_id=1, source_target_pairs={{0,2},{1,3},{2,0},{3,1},{4,6},{5,7},{6,4},{7,5},{8,10},{9,11},{10,... | collective-permute-start | bytes 786440 | tf_op jit(solution)/shard_map/ppermute | solution.py:90
  82.7 13.8 %collective-permute-start.20 = (bf16[2,2,128,1024]{3,2,1,0:T(8,128)(2,1)}, bf16[2,2,128,1024]{3,2,1,0:T(8,128)(2,1)}, u32[]{:S(2)}, u32[]{:S(2)}) collective-permute-start(bf16[2,2,128,1024]{3,2,1,0:T(8,128)(2,1)} %pad_maximum_fusion.7), channel_id=1, source_target_pairs={{0,1},{1,0},{2,3},{3,2},{4,5},{5,4},{6,7},{7,6},{8,9},{9,8},{10,11... | collective-permute-start | bytes 3145736 | tf_op jit(solution)/shard_map/ppermute | solution.py:90
  96.2 150.7 %reduce-scatter.5.cloned.1.call-start = ((), (), s32[]{:S(2)}) async-start(), calls=%async_computation.5 | async-start | bytes 1638400 | tf_op jit(solution)/shard_map/reduce_scatter | solution.py:101
  141.6 125.4 %reduce-scatter.3.cloned.1.call-start = ((), (), s32[]{:S(2)}) async-start(), calls=%async_computation.4 | async-start | bytes 3276800 | tf_op jit(solution)/shard_map/reduce_scatter | solution.py:101
  148.9 12.5 %collective-permute-start.23 = (bf16[128,1024]{1,0:T(8,128)(2,1)S(1)}, bf16[128,1024]{1,0:T(8,128)(2,1)S(1)}, u32[]{:S(2)}, u32[]{:S(2)}) collective-permute-start(bf16[128,1024]{1,0:T(8,128)(2,1)S(1)} %get-tuple-element.81), channel_id=1, source_target_pairs={{0,4},{1,5},{2,6},{3,7},{4,0},{5,1},{6,2},{7,3},{8,12},{9,13},{10,... | collective-permute-start | bytes 786440 | tf_op jit(solution)/shard_map/ppermute | solution.py:90
  165.9 18.5 %collective-permute-start.13 = (bf16[2,2,128,1024]{3,2,1,0:T(8,128)(2,1)S(1)}, bf16[2,2,128,1024]{3,2,1,0:T(8,128)(2,1)}, u32[]{:S(2)}, u32[]{:S(2)}) collective-permute-start(bf16[2,2,128,1024]{3,2,1,0:T(8,128)(2,1)S(1)} %dynamic-slice_bitcast_fusion.1), channel_id=1, source_target_pairs={{0,1},{1,0},{2,3},{3,2},{4,5},{5,4},{6,7},{7,6},{8,9},{9,8},{10,11... | collective-permute-start | bytes 3145736 | tf_op jit(solution)/shard_map/ppermute | solution.py:90
  170.9 18.8 %collective-permute-start.26 = (bf16[2,128,1024]{2,1,0:T(8,128)(2,1)S(1)}, bf16[2,128,1024]{2,1,0:T(8,128)(2,1)}, u32[]{:S(2)}, u32[]{:S(2)}) collective-permute-start(bf16[2,128,1024]{2,1,0:T(8,128)(2,1)S(1)} %pad_maximum_fusion.17), channel_id=1, source_target_pairs={{0,1},{1,0},{2,3},{3,2},{4,5},{5,4},{6,7},{7,6},{8,9},{9,8},{10,11... | collective-permute-start | bytes 1572872 | tf_op jit(solution)/shard_map/ppermute | solution.py:90
  187.3 82.5 %collective-permute-start.14 = (bf16[128,1024]{1,0:T(8,128)(2,1)}, bf16[128,1024]{1,0:T(8,128)(2,1)}, u32[]{:S(2)}, u32[]{:S(2)}) collective-permute-start(bf16[128,1024]{1,0:T(8,128)(2,1)} %get-tuple-element.84), channel_id=1, source_target_pairs={{0,6},{1,7},{2,4},{3,5},{4,2},{5,3},{6,0},{7,1},{8,14},{9,15},{10,... | collective-permute-start | bytes 786440 | tf_op jit(solution)/shard_map/ppermute | solution.py:90
  213.6 13.2 %collective-permute-start.38 = (bf16[4,128,256]{1,2,0:T(8,128)(2,1)}, bf16[4,128,256]{1,2,0:T(8,128)(2,1)}, u32[]{:S(2)}, u32[]{:S(2)}) collective-permute-start(bf16[4,128,256]{1,2,0:T(8,128)(2,1)} %bitcast.118), channel_id=1, source_target_pairs={{0,4},{1,5},{2,6},{3,7},{4,0},{5,1},{6,2},{7,3},{8,12},{9,13},{10,... | collective-permute-start | bytes 786440 | tf_op jit(solution)/shard_map/ppermute | solution.py:90
  218.5 21.8 %collective-permute-start.34 = (bf16[4,128,512]{2,1,0:T(8,128)(2,1)}, bf16[4,128,512]{2,1,0:T(8,128)(2,1)S(1)}, u32[]{:S(2)}, u32[]{:S(2)}) collective-permute-start(bf16[4,128,512]{2,1,0:T(8,128)(2,1)} %dynamic-slice_bitcast_fusion.2), channel_id=1, source_target_pairs={{0,4},{1,5},{2,6},{3,7},{4,0},{5,1},{6,2},{7,3},{8,12},{9,13},{10,... | collective-permute-start | bytes 1572872 | tf_op jit(solution)/shard_map/ppermute | solution.py:90
  235.7 34.0 %collective-permute-start.15 = (bf16[128,1024]{1,0:T(8,128)(2,1)}, bf16[128,1024]{1,0:T(8,128)(2,1)}, u32[]{:S(2)}, u32[]{:S(2)}) collective-permute-start(bf16[128,1024]{1,0:T(8,128)(2,1)} %get-tuple-element.86), channel_id=1, source_target_pairs={{0,4},{1,5},{2,6},{3,7},{4,0},{5,1},{6,2},{7,3},{8,12},{9,13},{10,... | collective-permute-start | bytes 786440 | tf_op jit(solution)/shard_map/ppermute | solution.py:90
  244.8 13.3 %collective-permute-start.37 = (bf16[128,512]{1,0:T(8,128)(2,1)}, bf16[128,512]{1,0:T(8,128)(2,1)}, u32[]{:S(2)}, u32[]{:S(2)}) collective-permute-start(bf16[128,512]{1,0:T(8,128)(2,1)} %get-tuple-element.106), channel_id=1, source_target_pairs={{0,24},{1,25},{2,26},{3,27},{4,28},{5,29},{6,30},{7,31},{8,16},{9,... | collective-permute-start | bytes 393224 | tf_op jit(solution)/shard_map/ppermute | solution.py:90
  250.0 19.7 %collective-permute-start.16 = (bf16[128,1024]{1,0:T(8,128)(2,1)}, bf16[128,1024]{1,0:T(8,128)(2,1)}, u32[]{:S(2)}, u32[]{:S(2)}) collective-permute-start(bf16[128,1024]{1,0:T(8,128)(2,1)} %get-tuple-element.85), channel_id=1, source_target_pairs={{0,2},{1,3},{2,0},{3,1},{4,6},{5,7},{6,4},{7,5},{8,10},{9,11},{10,... | collective-permute-start | bytes 786440 | tf_op jit(solution)/shard_map/ppermute | solution.py:90
  (105 other events, 740.2 us)
Sparse Core Ops, SparseCore 0:
  38.0 54.9 all-gather.2
  96.3 34.4 all-gather.4
  141.8 30.3 reduce-scatter.4
  184.5 55.7 reduce-scatter.2

commit v2 on v1

--- a/solution.py
+++ b/solution.py
@@ -139,7 +139,7 @@
         array = ordered(
             ordered(array, row, self.row, 0), ordered(pair, both, self.row, 0), self.pair, 0
         )
-        array = ordered(array, self.swap(array, self.core_mask), self.core, 2)
+        array = ordered(array, self.swap(array, self.core_mask), self.core, 0)
         return array.reshape((-1,) + array.shape[4:])
 
     def halve(self, array, mask, bit, axis):
@@ -153,7 +153,7 @@
 
     def scatter_group(self, array):
         array = array.reshape((2, 2, 2, -1) + array.shape[1:])
-        array = self.halve(array, self.core_mask, self.core, 2).astype(LOW)
+        array = self.halve(array, self.core_mask, self.core, 0).astype(LOW)
 
         def part(pair, row):
             return pick(pick(array, pair, 0), row, 0)

time: 288 us -> 288 us (level)
  waiting for transfers between devices: 97.9 us -> 103 us
  local copies, waits for them, and re-layouts: 35 us -> 31.4 us
  starting transfers between devices: 47.5 us -> 44.6 us
    ppermute x44, waiting for transfers between devices: 80.9 us -> 85.9 us  [swap(): lax.ppermute(array, AXES, [(i, i ^ mask) for i in range(self.devices)])]
    ppermute x44, starting transfers between devices: 47.1 us -> 44.2 us  [swap(): lax.ppermute(array, AXES, [(i, i ^ mask) for i in range(self.devices)])]
  transfers between devices with their start and end apart: 48 -> 48, of which waited for: 21 -> 20; matrix products, arithmetic and copies ran while one was open for 35% -> 35% of each run, Pallas kernels for 0% -> 0%
where the time goes in v2:
time: 288 us; the launch traced here: 284 us
  waiting for transfers between devices  103 us (36%)
  matrix products  46.2 us (16%)
  starting transfers between devices  44.6 us (15%)
  other arithmetic  42.6 us (15%)
  local copies, waits for them, and re-layouts  31.4 us (11%)
  between operations  15.7 us (5%)
    ppermute x44, waiting for transfers between devices, swap(): lax.ppermute(array, AXES, [(i, i ^ mask) for i in range(self.devices)])  85.9 us
    ppermute x44, starting transfers between devices, swap(): lax.ppermute(array, AXES, [(i, i ^ mask) for i in range(self.devices)])  44.2 us
    dot_general x4, matrix products, matmul_rows(): lax.dot_general(left, right, (((0,), (0,)), ((), ())), preferred_element_...  19.9 us
    all_gather x2, waiting for transfers between devices, gather_lines(): lax.all_gather(array, 'dp', axis=0, tiled=True, axis_index_groups=self.gr...  17.1 us
    another operation x21, other arithmetic, ordered(): jnp.stack([jnp.where(first, mine, other), jnp.where(first, other, mine)],...  16.9 us
    dot_general x4, matrix products, matmul(): return jnp.dot(left, right, preferred_element_type=FULL)  12.5 us
    unnamed x162, local copies, waits for them, and re-layouts  12.3 us
    squeeze x11, local copies, waits for them, and re-layouts, pick(): return lax.dynamic_index_in_dim(array, index, axis, keepdims=False)  8.58 us
  transfers between devices with their start and end apart: 48, of which 20 were waited for; matrix products, arithmetic and copies ran while one was open for 35% of the time, Pallas kernels for 0%

profile of v2, /device:TPU:0, one launch (start us, length us, event | category | flops | bytes accessed | tf_op | source)
XLA Modules:
  0.0 283.6 jit_solution(13709473035280445470)
XLA Ops:
  9.1 3.1 %collective-permute-start.2 = (bf16[128,768]{1,0:T(8,128)(2,1)S(1)}, bf16[128,768]{1,0:T(8,128)(2,1)}, u32[]{:S(2)}, u32[]{:S(2)}) collective-permute-start(bf16[128,768]{1,0:T(8,128)(2,1)S(1)} %pad_maximum_fusion.24), channel_id=1, source_target_pairs={{0,8},{1,9},{2,10},{3,11},{4,12},{5,13},{6,14},{7,15},{8,0},{9,1},... | collective-permute-start | bytes 589832 | tf_op jit(solution)/shard_map/ppermute | solution.py:90
  12.2 2.6 collective-permute-start.3
  22.4 7.1 %collective-permute-done.3 = bf16[128,768]{1,0:T(8,128)(2,1)} collective-permute-done((bf16[128,768]{1,0:T(8,128)(2,1)S(1)}, bf16[128,768]{1,0:T(8,128)(2,1)}, u32[]{:S(2)}, u32[]{:S(2)}) %collective-permute-start.3) | collective-permute-done | bytes 196640 | tf_op jit(solution)/shard_map/ppermute | solution.py:90
  40.1 7.9 %collective-permute-done.5 = bf16[4,128,768]{2,1,0:T(8,128)(2,1)} collective-permute-done((bf16[4,128,768]{2,1,0:T(8,128)(2,1)S(1)}, bf16[4,128,768]{2,1,0:T(8,128)(2,1)}, u32[]{:S(2)}, u32[]{:S(2)}) %collective-permute-start.5) | collective-permute-done | bytes 786464 | tf_op jit(solution)/shard_map/ppermute | solution.py:90
  60.5 12.6 %collective-permute-done.17 = bf16[128,1024]{1,0:T(8,128)(2,1)} collective-permute-done((bf16[128,1024]{1,0:T(8,128)(2,1)S(1)}, bf16[128,1024]{1,0:T(8,128)(2,1)}, u32[]{:S(2)}, u32[]{:S(2)}) %collective-permute-start.17) | collective-permute-done | bytes 262176 | tf_op jit(solution)/shard_map/ppermute | solution.py:90
  82.7 8.3 %collective-permute-done.8 = bf16[128,1024]{1,0:T(8,128)(2,1)S(1)} collective-permute-done((bf16[128,1024]{1,0:T(8,128)(2,1)S(1)}, bf16[128,1024]{1,0:T(8,128)(2,1)S(1)}, u32[]{:S(2)}, u32[]{:S(2)}) %collective-permute-start.8) | collective-permute-done | bytes 262176 | tf_op jit(solution)/shard_map/ppermute | solution.py:90
  102.2 5.3 %fusion.79 = f32[1024,1280]{1,0:T(8,128)S(1)} fusion(bf16[1024,1024]{1,0:T(8,128)(2,1)} %bitcast.337, bf16[1024,1280]{1,0:T(8,128)(2,1)} %all-gather.3.cloned.1.call-done), kind=kOutput, calls=%fused_computation.241 | convolution fusion | flops 2684354560 | bytes 9961472 | tf_op jit(solution)/shard_map/dot_general | solution.py:14
  110.7 3.0 %convolution_convert_fusion.3 = bf16[1024,640]{1,0:T(8,128)(2,1)} fusion(bf16[1024,1024]{1,0:T(8,128)(2,1)S(1)} %bitcast.340, bf16[1024,640]{1,0:T(8,128)(2,1)S(1)} %multiply_convert_fusion.2), kind=kOutput, calls=%fused_computation.34 | convolution fusion | flops 1342832640 | bytes 4718592 | tf_op jit(solution)/shard_map/dot_general | solution.py:22
  113.7 17.1 %all-gather.5.cloned.1.call-done = bf16[1024,640]{1,0:T(8,128)(2,1)} async-done(((bf16[256,640]{1,0:T(8,128)(2,1)}), bf16[1024,640]{1,0:T(8,128)(2,1)}) %all-gather.5.cloned.1.call-update) | async-done | bytes 1310736 | tf_op jit(solution)/shard_map/all_gather | solution.py:98
  130.8 6.0 %multiply_convert_fusion.1 = (bf16[1024,640]{1,0:T(8,128)(2,1)S(1)}, bf16[1024,640]{1,0:T(8,128)(2,1)S(1)}) fusion(f32[1024,1280]{1,0:T(8,128)} %copy-done.6, bf16[1024,1024]{1,0:T(8,128)(2,1)} %bitcast.339, bf16[1024,640]{1,0:T(8,128)(2,1)} %all-gather.5.cloned.1.call-done), kind=kOutput, calls=%fused_computation.13 | convolution fusion | flops 1350696960 | bytes 11272192 | tf_op jit(solution)/shard_map/dot_general | solution.py:14
  136.8 3.1 %convolution_convert_fusion.1 = bf16[1024,1024]{1,0:T(8,128)(2,1)S(1)} fusion(bf16[1024,1280]{1,0:T(8,128)(2,1)S(1)} %copy-done.72, bf16[1024,640]{1,0:T(8,128)(2,1)S(1)} %get-tuple-element.66, bf16[1024,640]{1,0:T(8,128)(2,1)S(1)} %get-tuple-element.65), kind=kOutput, calls=%fused_computation.32 | convolution fusion | flops 2690646016 | bytes 7340032 | tf_op jit(solution)/shard_map/dot_general | solution.py:18
  141.7 2.7 collective-permute-done.21
  150.0 6.6 %collective-permute-done.22 = bf16[128,1024]{1,0:T(8,128)(2,1)S(1)} collective-permute-done((bf16[128,1024]{1,0:T(8,128)(2,1)S(1)}, bf16[128,1024]{1,0:T(8,128)(2,1)S(1)}, u32[]{:S(2)}, u32[]{:S(2)}) %collective-permute-start.22) | collective-permute-done | bytes 262176 | tf_op jit(solution)/shard_map/ppermute | solution.py:90
  156.6 4.8 %collective-permute-done.23 = bf16[128,1024]{1,0:T(8,128)(2,1)S(1)} collective-permute-done((bf16[128,1024]{1,0:T(8,128)(2,1)S(1)}, bf16[128,1024]{1,0:T(8,128)(2,1)S(1)}, u32[]{:S(2)}, u32[]{:S(2)}) %collective-permute-start.23) | collective-permute-done | bytes 262176 | tf_op jit(solution)/shard_map/ppermute | solution.py:90
  166.0 4.8 %collective-permute-done.25 = bf16[128,1024]{1,0:T(8,128)(2,1)S(1)} collective-permute-done((bf16[128,1024]{1,0:T(8,128)(2,1)S(1)}, bf16[128,1024]{1,0:T(8,128)(2,1)S(1)}, u32[]{:S(2)}, u32[]{:S(2)}) %collective-permute-start.25) | collective-permute-done | bytes 262176 | tf_op jit(solution)/shard_map/ppermute | solution.py:90
  171.7 13.3 %convolution_convert_fusion = bf16[1024,1280]{1,0:T(8,128)(2,1)} fusion(bf16[1024,1024]{1,0:T(8,128)(2,1)S(1)} %bitcast.338, bf16[1024,640]{1,0:T(8,128)(2,1)S(1)} %copy-done.78, bf16[1024,640]{1,0:T(8,128)(2,1)S(1)} %copy-done.76), kind=kOutput, calls=%fused_computation.7 | convolution fusion | flops 2690908160 | bytes 7340032 | tf_op jit(solution)/shard_map/dot_general | solution.py:22
  202.8 3.1 %convolution_convert_fusion.5 = bf16[1024,512]{1,0:T(8,128)(2,1)} fusion(bf16[512,1024]{1,0:T(8,128)(2,1)} %copy-done.27, bf16[512,128]{0,1:T(8,128)(2,1)} %bitcast.372, bf16[512,128]{0,1:T(8,128)(2,1)S(1)} %bitcast.364, bf16[512,256]{0,1:T(8,128)(2,1)} %bitcast.360), kind=kOutput, calls=%fused_computation.37 | convolution fusion | flops 538968064 | bytes 2621440 | tf_op jit(solution)/shard_map/dot_general | solution.py:22
  221.1 3.7 %collective-permute-done.33 = f32[2176]{0:T(1024)S(1)} collective-permute-done((f32[2176]{0:T(1024)S(1)}, f32[2176]{0:T(1024)S(1)}, u32[]{:S(2)}, u32[]{:S(2)}) %collective-permute-start.33) | collective-permute-done | bytes 8736 | tf_op jit(solution)/shard_map/ppermute | solution.py:90
  227.5 3.4 %collective-permute-start.41 = (bf16[128,256]{0,1:T(8,128)(2,1)S(1)}, bf16[128,256]{0,1:T(8,128)(2,1)S(1)}, u32[]{:S(2)}, u32[]{:S(2)}) collective-permute-start(bf16[128,256]{0,1:T(8,128)(2,1)S(1)} %get-tuple-element.135), channel_id=1, source_target_pairs={{0,24},{1,25},{2,26},{3,27},{4,28},{5,29},{6,30},{7,31},{8,16},{9,... | collective-permute-start | bytes 196616 | tf_op jit(solution)/shard_map/ppermute | solution.py:90
  231.5 4.4 %collective-permute-done.39 = bf16[128,256]{0,1:T(8,128)(2,1)S(1)} collective-permute-done((bf16[128,256]{0,1:T(8,128)(2,1)S(1)}, bf16[128,256]{0,1:T(8,128)(2,1)S(1)}, u32[]{:S(2)}, u32[]{:S(2)}) %collective-permute-start.39) | collective-permute-done | bytes 65568 | tf_op jit(solution)/shard_map/ppermute | solution.py:90
  240.8 4.0 %collective-permute-start.35 = (bf16[128,512]{1,0:T(8,128)(2,1)}, bf16[128,512]{1,0:T(8,128)(2,1)S(1)}, u32[]{:S(2)}, u32[]{:S(2)}) collective-permute-start(bf16[128,512]{1,0:T(8,128)(2,1)} %get-tuple-element.105), channel_id=1, source_target_pairs={{0,8},{1,9},{2,10},{3,11},{4,12},{5,13},{6,14},{7,15},{8,0},{9,1},... | collective-permute-start | bytes 393224 | tf_op jit(solution)/shard_map/ppermute | solution.py:90
  250.3 5.9 %collective-permute-done.36 = bf16[128,512]{1,0:T(8,128)(2,1)} collective-permute-done((bf16[128,512]{1,0:T(8,128)(2,1)}, bf16[128,512]{1,0:T(8,128)(2,1)}, u32[]{:S(2)}, u32[]{:S(2)}) %collective-permute-start.36) | collective-permute-done | bytes 131104 | tf_op jit(solution)/shard_map/ppermute | solution.py:90
  259.0 2.5 collective-permute-done.43
  270.3 4.6 %collective-permute-done.42 = bf16[128,1280]{1,0:T(8,128)(2,1)S(1)} collective-permute-done((bf16[128,1280]{1,0:T(8,128)(2,1)S(1)}, bf16[128,1280]{1,0:T(8,128)(2,1)S(1)}, u32[]{:S(2)}, u32[]{:S(2)}) %collective-permute-start.42) | collective-permute-done | bytes 327712 | tf_op jit(solution)/shard_map/ppermute | solution.py:90
  (377 shorter events, 128.2 us)
Async XLA Ops:
  7.2 95.0 %all-gather.3.cloned.1.call-start = ((), (), s32[]{:S(2)}) async-start(), calls=%async_computation.2 | async-start | bytes 3276800 | tf_op jit(solution)/shard_map/all_gather | solution.py:98
  9.1 12.3 %collective-permute-start.2 = (bf16[128,768]{1,0:T(8,128)(2,1)S(1)}, bf16[128,768]{1,0:T(8,128)(2,1)}, u32[]{:S(2)}, u32[]{:S(2)}) collective-permute-start(bf16[128,768]{1,0:T(8,128)(2,1)S(1)} %pad_maximum_fusion.24), channel_id=1, source_target_pairs={{0,8},{1,9},{2,10},{3,11},{4,12},{5,13},{6,14},{7,15},{8,0},{9,1},... | collective-permute-start | bytes 589832 | tf_op jit(solution)/shard_map/ppermute | solution.py:90
  12.2 17.3 %collective-permute-start.3 = (bf16[128,768]{1,0:T(8,128)(2,1)S(1)}, bf16[128,768]{1,0:T(8,128)(2,1)}, u32[]{:S(2)}, u32[]{:S(2)}) collective-permute-start(bf16[128,768]{1,0:T(8,128)(2,1)S(1)} %pad_maximum_fusion.24), channel_id=1, source_target_pairs={{0,16},{1,17},{2,18},{3,19},{4,20},{5,21},{6,22},{7,23},{8,24},{9,... | collective-permute-start | bytes 589832 | tf_op jit(solution)/shard_map/ppermute | solution.py:90
  14.8 15.6 %collective-permute-start.4 = (bf16[128,768]{1,0:T(8,128)(2,1)S(1)}, bf16[128,768]{1,0:T(8,128)(2,1)S(1)}, u32[]{:S(2)}, u32[]{:S(2)}) collective-permute-start(bf16[128,768]{1,0:T(8,128)(2,1)S(1)} %pad_maximum_fusion.24), channel_id=1, source_target_pairs={{0,24},{1,25},{2,26},{3,27},{4,28},{5,29},{6,30},{7,31},{8,16},{9,... | collective-permute-start | bytes 589832 | tf_op jit(solution)/shard_map/ppermute | solution.py:90
  14.8 17.2 %collective-permute-start = (bf16[128,1024]{1,0:T(8,128)(2,1)}, bf16[128,1024]{1,0:T(8,128)(2,1)}, u32[]{:S(2)}, u32[]{:S(2)}) collective-permute-start(bf16[128,1024]{1,0:T(8,128)(2,1)} %param.15), channel_id=1, source_target_pairs={{0,2},{1,3},{2,0},{3,1},{4,6},{5,7},{6,4},{7,5},{8,10},{9,11},{10,... | collective-permute-start | bytes 786440 | tf_op jit(solution)/shard_map/ppermute | solution.py:90
  19.1 14.7 %collective-permute-start.12 = (bf16[128,1920]{1,0:T(8,128)(2,1)S(1)}, bf16[128,1920]{1,0:T(8,128)(2,1)S(1)}, u32[]{:S(2)}, u32[]{:S(2)}) collective-permute-start(bf16[128,1920]{1,0:T(8,128)(2,1)S(1)} %pad_maximum_fusion.20), channel_id=1, source_target_pairs={{0,4},{1,5},{2,6},{3,7},{4,0},{5,1},{6,2},{7,3},{8,12},{9,13},{10,... | collective-permute-start | bytes 1474568 | tf_op jit(solution)/shard_map/ppermute | solution.py:90
  30.5 17.6 %collective-permute-start.5 = (bf16[4,128,768]{2,1,0:T(8,128)(2,1)S(1)}, bf16[4,128,768]{2,1,0:T(8,128)(2,1)}, u32[]{:S(2)}, u32[]{:S(2)}) collective-permute-start(bf16[4,128,768]{2,1,0:T(8,128)(2,1)S(1)} %bitcast_dynamic-update-slice_fusion), channel_id=1, source_target_pairs={{0,4},{1,5},{2,6},{3,7},{4,0},{5,1},{6,2},{7,3},{8,12},{9,13},{10,... | collective-permute-start | bytes 2359304 | tf_op jit(solution)/shard_map/ppermute | solution.py:90
  37.9 92.9 %all-gather.5.cloned.1.call-start = ((), (), s32[]{:S(2)}) async-start(), calls=%async_computation.3 | async-start | bytes 1638400 | tf_op jit(solution)/shard_map/all_gather | solution.py:98
  56.1 17.9 %collective-permute-start.18 = (bf16[128,1024]{1,0:T(8,128)(2,1)S(1)}, bf16[128,1024]{1,0:T(8,128)(2,1)}, u32[]{:S(2)}, u32[]{:S(2)}) collective-permute-start(bf16[128,1024]{1,0:T(8,128)(2,1)S(1)} %copy-done.15), channel_id=1, source_target_pairs={{0,4},{1,5},{2,6},{3,7},{4,0},{5,1},{6,2},{7,3},{8,12},{9,13},{10,... | collective-permute-start | bytes 786440 | tf_op jit(solution)/shard_map/ppermute | solution.py:90
  57.6 16.5 %collective-permute-start.19 = (bf16[128,1024]{1,0:T(8,128)(2,1)S(1)}, bf16[128,1024]{1,0:T(8,128)(2,1)}, u32[]{:S(2)}, u32[]{:S(2)}) collective-permute-start(bf16[128,1024]{1,0:T(8,128)(2,1)S(1)} %copy-done.15), channel_id=1, source_target_pairs={{0,6},{1,7},{2,4},{3,5},{4,2},{5,3},{6,0},{7,1},{8,14},{9,15},{10,... | collective-permute-start | bytes 786440 | tf_op jit(solution)/shard_map/ppermute | solution.py:90
  58.1 14.9 %collective-permute-start.17 = (bf16[128,1024]{1,0:T(8,128)(2,1)S(1)}, bf16[128,1024]{1,0:T(8,128)(2,1)}, u32[]{:S(2)}, u32[]{:S(2)}) collective-permute-start(bf16[128,1024]{1,0:T(8,128)(2,1)S(1)} %copy-done.15), channel_id=1, source_target_pairs={{0,2},{1,3},{2,0},{3,1},{4,6},{5,7},{6,4},{7,5},{8,10},{9,11},{10,... | collective-permute-start | bytes 786440 | tf_op jit(solution)/shard_map/ppermute | solution.py:90
  59.9 17.7 %collective-permute-start.7 = (bf16[128,1024]{1,0:T(8,128)(2,1)S(1)}, bf16[128,1024]{1,0:T(8,128)(2,1)S(1)}, u32[]{:S(2)}, u32[]{:S(2)}) collective-permute-start(bf16[128,1024]{1,0:T(8,128)(2,1)S(1)} %fusion.49), channel_id=1, source_target_pairs={{0,2},{1,3},{2,0},{3,1},{4,6},{5,7},{6,4},{7,5},{8,10},{9,11},{10,... | collective-permute-start | bytes 786440 | tf_op jit(solution)/shard_map/ppermute | solution.py:90
  77.9 13.1 %collective-permute-start.8 = (bf16[128,1024]{1,0:T(8,128)(2,1)S(1)}, bf16[128,1024]{1,0:T(8,128)(2,1)S(1)}, u32[]{:S(2)}, u32[]{:S(2)}) collective-permute-start(bf16[128,1024]{1,0:T(8,128)(2,1)S(1)} %multiply_convert_fusion.4), channel_id=1, source_target_pairs={{0,2},{1,3},{2,0},{3,1},{4,6},{5,7},{6,4},{7,5},{8,10},{9,11},{10,... | collective-permute-start | bytes 786440 | tf_op jit(solution)/shard_map/ppermute | solution.py:90
  82.7 13.8 %collective-permute-start.20 = (bf16[2,2,128,1024]{3,2,1,0:T(8,128)(2,1)}, bf16[2,2,128,1024]{3,2,1,0:T(8,128)(2,1)}, u32[]{:S(2)}, u32[]{:S(2)}) collective-permute-start(bf16[2,2,128,1024]{3,2,1,0:T(8,128)(2,1)} %pad_maximum_fusion.7), channel_id=1, source_target_pairs={{0,1},{1,0},{2,3},{3,2},{4,5},{5,4},{6,7},{7,6},{8,9},{9,8},{10,11... | collective-permute-start | bytes 3145736 | tf_op jit(solution)/shard_map/ppermute | solution.py:90
  96.2 151.2 %reduce-scatter.5.cloned.1.call-start = ((), (), s32[]{:S(2)}) async-start(), calls=%async_computation.5 | async-start | bytes 1638400 | tf_op jit(solution)/shard_map/reduce_scatter | solution.py:101
  141.6 125.1 %reduce-scatter.3.cloned.1.call-start = ((), (), s32[]{:S(2)}) async-start(), calls=%async_computation.4 | async-start | bytes 3276800 | tf_op jit(solution)/shard_map/reduce_scatter | solution.py:101
  148.9 12.5 %collective-permute-start.23 = (bf16[128,1024]{1,0:T(8,128)(2,1)S(1)}, bf16[128,1024]{1,0:T(8,128)(2,1)S(1)}, u32[]{:S(2)}, u32[]{:S(2)}) collective-permute-start(bf16[128,1024]{1,0:T(8,128)(2,1)S(1)} %get-tuple-element.81), channel_id=1, source_target_pairs={{0,4},{1,5},{2,6},{3,7},{4,0},{5,1},{6,2},{7,3},{8,12},{9,13},{10,... | collective-permute-start | bytes 786440 | tf_op jit(solution)/shard_map/ppermute | solution.py:90
  165.9 19.1 %collective-permute-start.13 = (bf16[2,2,128,1024]{3,2,1,0:T(8,128)(2,1)S(1)}, bf16[2,2,128,1024]{3,2,1,0:T(8,128)(2,1)}, u32[]{:S(2)}, u32[]{:S(2)}) collective-permute-start(bf16[2,2,128,1024]{3,2,1,0:T(8,128)(2,1)S(1)} %dynamic-slice_bitcast_fusion.1), channel_id=1, source_target_pairs={{0,1},{1,0},{2,3},{3,2},{4,5},{5,4},{6,7},{7,6},{8,9},{9,8},{10,11... | collective-permute-start | bytes 3145736 | tf_op jit(solution)/shard_map/ppermute | solution.py:90
  171.7 18.7 %collective-permute-start.26 = (bf16[2,128,1024]{2,1,0:T(8,128)(2,1)}, bf16[2,128,1024]{2,1,0:T(8,128)(2,1)S(1)}, u32[]{:S(2)}, u32[]{:S(2)}) collective-permute-start(bf16[2,128,1024]{2,1,0:T(8,128)(2,1)} %pad_maximum_fusion.17), channel_id=1, source_target_pairs={{0,1},{1,0},{2,3},{3,2},{4,5},{5,4},{6,7},{7,6},{8,9},{9,8},{10,11... | collective-permute-start | bytes 1572872 | tf_op jit(solution)/shard_map/ppermute | solution.py:90
  188.0 79.9 %collective-permute-start.14 = (bf16[128,1024]{1,0:T(8,128)(2,1)}, bf16[128,1024]{1,0:T(8,128)(2,1)}, u32[]{:S(2)}, u32[]{:S(2)}) collective-permute-start(bf16[128,1024]{1,0:T(8,128)(2,1)} %get-tuple-element.84), channel_id=1, source_target_pairs={{0,6},{1,7},{2,4},{3,5},{4,2},{5,3},{6,0},{7,1},{8,14},{9,15},{10,... | collective-permute-start | bytes 786440 | tf_op jit(solution)/shard_map/ppermute | solution.py:90
  211.5 13.9 %collective-permute-start.38 = (bf16[4,128,256]{1,2,0:T(8,128)(2,1)}, bf16[4,128,256]{1,2,0:T(8,128)(2,1)}, u32[]{:S(2)}, u32[]{:S(2)}) collective-permute-start(bf16[4,128,256]{1,2,0:T(8,128)(2,1)} %bitcast.118), channel_id=1, source_target_pairs={{0,4},{1,5},{2,6},{3,7},{4,0},{5,1},{6,2},{7,3},{8,12},{9,13},{10,... | collective-permute-start | bytes 786440 | tf_op jit(solution)/shard_map/ppermute | solution.py:90
  216.1 22.7 %collective-permute-start.34 = (bf16[4,128,512]{2,1,0:T(8,128)(2,1)}, bf16[4,128,512]{2,1,0:T(8,128)(2,1)S(1)}, u32[]{:S(2)}, u32[]{:S(2)}) collective-permute-start(bf16[4,128,512]{2,1,0:T(8,128)(2,1)} %dynamic-slice_bitcast_fusion.2), channel_id=1, source_target_pairs={{0,4},{1,5},{2,6},{3,7},{4,0},{5,1},{6,2},{7,3},{8,12},{9,13},{10,... | collective-permute-start | bytes 1572872 | tf_op jit(solution)/shard_map/ppermute | solution.py:90
  235.8 32.1 %collective-permute-start.15 = (bf16[128,1024]{1,0:T(8,128)(2,1)}, bf16[128,1024]{1,0:T(8,128)(2,1)}, u32[]{:S(2)}, u32[]{:S(2)}) collective-permute-start(bf16[128,1024]{1,0:T(8,128)(2,1)} %get-tuple-element.86), channel_id=1, source_target_pairs={{0,4},{1,5},{2,6},{3,7},{4,0},{5,1},{6,2},{7,3},{8,12},{9,13},{10,... | collective-permute-start | bytes 786440 | tf_op jit(solution)/shard_map/ppermute | solution.py:90
  249.0 18.9 %collective-permute-start.16 = (bf16[128,1024]{1,0:T(8,128)(2,1)}, bf16[128,1024]{1,0:T(8,128)(2,1)}, u32[]{:S(2)}, u32[]{:S(2)}) collective-permute-start(bf16[128,1024]{1,0:T(8,128)(2,1)} %get-tuple-element.85), channel_id=1, source_target_pairs={{0,2},{1,3},{2,0},{3,1},{4,6},{5,7},{6,4},{7,5},{8,10},{9,11},{10,... | collective-permute-start | bytes 786440 | tf_op jit(solution)/shard_map/ppermute | solution.py:90
  (105 other events, 756.6 us)
Sparse Core Ops, SparseCore 0:
  38.0 54.9 all-gather.2
  96.3 34.4 all-gather.4
  141.8 30.3 reduce-scatter.4
  185.2 55.8 reduce-scatter.2
